TPU v7x, 32 devices: a whole 2x2x4 slice. The times are simulated.
32 devices in a mesh: row: 4 (over z), col: 8 (over y, x, core).
Axes of the slice: x: 2, y: 2, z: 4, core: 2. Of those that a mesh axis runs over, the one named last changes fastest.
Arguments:
- amplitudes: bfloat16 [8, 1024, 3072], P('row', None, 'col'), may hold values from -6 to 6
- integrals: bfloat16 [32, 1024, 1024], P('row', 'col'), may hold values from -0.1875 to 0.1875
- source_pair: int32 [32], P('row'), may hold values from 0 to 7, as said below
- target_pair: int32 [32], P('row'), may hold values from 0 to 1
- symmetry_mask: int32 [32], P('row'), may hold values from 0 to 1
Outputs:
- residual: float32 [8, 1024, 3072], P('row', None, 'col')
Inputs may be any that keep to these rules, and one draw needn't show every extreme that they name: The tile pairs owned by one owner group (source_pair // 2) are named by exactly 2 of the 8 slots of every owner group, and, for every position j, the 8 slots at position j within their owner groups (one per owner group) name each owner group's tile pairs exactly once.
All inputs are finite; a program needn't handle non-finite values.
Results may differ from a plain program's by a relative error of at most 0.0029.
Values may be sent and summed in bfloat16 or wider, within the bound.
A program may use at most 128 MiB of HBM per device.

v0:
```python
import functools

import jax
import jax.numpy as jnp
from jax import lax
from jax.experimental import pallas as pl
from jax.experimental.pallas import tpu as pltpu
from jax.sharding import PartitionSpec as P

MESH = pl.DeviceIdType.MESH
CHUNKS = 4
ROW_TILE = 256


def line_kernel(groups, source, target, mask, amp, integ, out, table, own, u1, u2, u3, d1, d2, d3,
                local_sem, isend, irecv, usend, urecv, dsend, drecv):
    z = lax.axis_index("row")
    col = lax.axis_index("col")
    core, x, y = col % 2, (col // 2) % 2, col // 4
    slots, rows, _ = integ.shape
    half = slots // 2
    pairs, depth, _ = amp.shape

    def place(py, px, pc):
        return (py * 2 + px) * 2 + pc

    sib, xn, yn = place(y, x, 1 - core), place(y, 1 - x, core), place(1 - y, x, core)
    diag = place(1 - y, 1 - x, core)
    low, high = z > 0, z < groups - 1

    barrier = pltpu.get_barrier_semaphore()
    for partner in (sib, xn, yn):
        pl.semaphore_signal(barrier, inc=1, device_id=(z, partner), device_id_type=MESH)

    @pl.when(low)
    def _():
        pl.semaphore_signal(barrier, inc=1, device_id=(z - 1, col), device_id_type=MESH)

    @pl.when(high)
    def _():
        pl.semaphore_signal(barrier, inc=1, device_id=(z + 1, col), device_id_type=MESH)

    own_rows = table.at[:, pl.ds(col * rows, rows), :]
    fetch_i = pltpu.make_async_copy(integ, own_rows, local_sem.at[0])
    fetch_a = pltpu.make_async_copy(amp, own, local_sem.at[1])
    fetch_i.start()
    fetch_a.start()
    pl.semaphore_wait(barrier, 3 + jnp.where(low, 1, 0) + jnp.where(high, 1, 0))

    per_tile = CHUNKS // pairs
    chunk_rows = depth // per_tile

    def piece(ref, q):
        return ref.at[q // per_tile, pl.ds((q % per_tile) * chunk_rows, chunk_rows), :]

    ups, downs = (own, u1, u2, u3), (own, d1, d2, d3)

    def up(d, q):
        src = amp if d == 1 else ups[d - 1]
        i = (d - 1) * CHUNKS + q
        return pltpu.make_async_remote_copy(
            piece(src, q), piece(ups[d], q), usend.at[i], urecv.at[i],
            device_id=(z + 1, col), device_id_type=MESH)

    def down(d, q):
        src = amp if d == 1 else downs[d - 1]
        i = (d - 1) * CHUNKS + q
        return pltpu.make_async_remote_copy(
            piece(src, q), piece(downs[d], q), dsend.at[i], drecv.at[i],
            device_id=(z - 1, col), device_id_type=MESH)

    def rows_copy(i, block, first, count, partner):
        window = table.at[pl.ds(first, count), pl.ds(block * rows, rows), :]
        src = integ.at[pl.ds(first, count)] if i < 5 else window
        return pltpu.make_async_remote_copy(
            src, window, isend.at[i], irecv.at[i], device_id=(z, partner), device_id_type=MESH)

    moves = [
        rows_copy(0, col, 0, slots, sib),
        rows_copy(1, col, half, half, xn),
        rows_copy(2, col, 0, half, xn),
        rows_copy(3, col, 0, half, yn),
        rows_copy(4, col, half, half, yn),
        rows_copy(5, yn, 0, half, xn),
        rows_copy(6, xn, half, half, yn),
        rows_copy(7, xn, half, half, sib),
        rows_copy(8, xn, 0, half, sib),
        rows_copy(9, yn, 0, half, sib),
        rows_copy(10, yn, half, half, sib),
        rows_copy(11, diag, 0, half, sib),
        rows_copy(12, diag, half, half, sib),
    ]

    for q in range(CHUNKS):
        @pl.when(low)
        def _():
            down(1, q).start()

        @pl.when(high)
        def _():
            up(1, q).start()

    for i in (1, 3, 2, 4, 0):
        moves[i].start()

    def pass_on(d, q):
        @pl.when(z >= d)
        def _():
            up(d, q).wait_recv()
            if d < groups - 1:
                @pl.when(high)
                def _():
                    up(d + 1, q).start()

        @pl.when(z + d < groups)
        def _():
            down(d, q).wait_recv()
            if d < groups - 1:
                @pl.when(low)
                def _():
                    down(d + 1, q).start()

    out[...] = jnp.zeros_like(out)
    mid = CHUNKS // 2
    for q in range(mid):
        pass_on(1, q)
    moves[3].wait_recv()
    moves[5].start()
    moves[9].start()
    moves[1].wait_recv()
    moves[6].start()
    moves[7].start()
    for q in range(mid, CHUNKS):
        pass_on(1, q)
    moves[4].wait_recv()
    moves[10].start()
    moves[2].wait_recv()
    moves[8].start()
    for q in range(mid):
        pass_on(2, q)
    moves[5].wait_recv()
    moves[11].start()
    moves[6].wait_recv()
    moves[12].start()
    for q in range(mid, CHUNKS):
        pass_on(2, q)
    fetch_i.wait()
    fetch_a.wait()
    for i in (0, 7, 8, 9, 10, 11, 12):
        moves[i].wait_recv()

    def contract(tiles, group):
        first = jnp.int32(slots)
        last = jnp.int32(-1)
        for k in range(slots):
            match = source[k] // pairs == group
            first = jnp.where(match, jnp.minimum(first, k), first)
            last = jnp.where(match, jnp.maximum(last, k), last)
        for k in (first, last):
            k = jnp.clip(k, 0, slots - 1)
            tile = source[k] % pairs
            goal = jnp.where(mask[k] > 0, target[k], -1)

            @pl.loop(0, depth // ROW_TILE)
            def _(r):
                span = pl.ds(pl.multiple_of(r * ROW_TILE, ROW_TILE), ROW_TILE)
                product = jnp.dot(table[k, span, :], tiles[tile], preferred_element_type=jnp.float32)
                product = product.astype(jnp.bfloat16).astype(jnp.float32)
                for p in range(pairs):
                    out[p, span, :] += jnp.where(goal == p, product, 0.0)

    contract(own, z)
    for d in range(1, groups):
        if d == groups - 1:
            for q in range(CHUNKS):
                pass_on(d, q)

        @pl.when(z >= d)
        def _():
            contract(ups[d], z - d)

        @pl.when(z + d < groups)
        def _():
            contract(downs[d], z + d)

    for move in moves:
        move.wait_send()
    for d in range(1, groups):
        for q in range(CHUNKS):
            @pl.when(high & (z >= d - 1))
            def _():
                up(d, q).wait_send()

            @pl.when(low & (z + d - 1 < groups))
            def _():
                down(d, q).wait_send()


def on_line(groups, amplitudes, integrals, source_pair, target_pair, symmetry_mask):
    pairs, depth, width = amplitudes.shape
    slots, rows, inner = integrals.shape
    across = depth // rows
    shard = pltpu.VMEM(amplitudes.shape, amplitudes.dtype)
    hops = (groups - 1) * CHUNKS
    return pl.pallas_call(
        functools.partial(line_kernel, groups),
        out_shape=jax.ShapeDtypeStruct((pairs, depth, width), jnp.float32),
        in_specs=[pl.BlockSpec(memory_space=pltpu.SMEM)] * 3 + [pl.BlockSpec(memory_space=pl.ANY)] * 2,
        out_specs=pl.BlockSpec(memory_space=pltpu.VMEM),
        scratch_shapes=[
            pltpu.VMEM((slots, rows * across, inner), integrals.dtype),
            shard, shard, shard, shard, shard, shard, shard,
            pltpu.SemaphoreType.DMA((2,)),
            pltpu.SemaphoreType.DMA((13,)),
            pltpu.SemaphoreType.DMA((13,)),
            pltpu.SemaphoreType.DMA((hops,)),
            pltpu.SemaphoreType.DMA((hops,)),
            pltpu.SemaphoreType.DMA((hops,)),
            pltpu.SemaphoreType.DMA((hops,)),
        ],
        compiler_params=pltpu.CompilerParams(
            collective_id=0, has_side_effects=True, vmem_limit_bytes=48 * 1024 * 1024
        ),
        cost_estimate=pl.CostEstimate(
            flops=2 * slots * depth * inner * width, bytes_accessed=16 * 1024 * 1024, transcendentals=0
        ),
    )(source_pair, target_pair, symmetry_mask, amplitudes, integrals)


def on_device(amplitudes, integrals, source_pair, target_pair, symmetry_mask):
    pairs = amplitudes.shape[0]
    tile_table = lax.all_gather(amplitudes, "row", axis=0, tiled=True)
    piece = lax.all_gather(integrals, "col", axis=1, tiled=True)
    total = [jnp.zeros(amplitudes.shape[1:], jnp.float32)] * pairs
    for slot in range(integrals.shape[0]):
        tile = lax.dynamic_index_in_dim(tile_table, source_pair[slot], 0, keepdims=False)
        product = jnp.dot(piece[slot], tile, preferred_element_type=jnp.float32).astype(jnp.bfloat16)
        goal = jnp.where(symmetry_mask[slot] > 0, target_pair[slot], -1)
        for p in range(pairs):
            total[p] += jnp.where(goal == p, product.astype(jnp.float32), 0.0)
    return jnp.stack(total)


def solution(mesh):
    placed = (P("row", None, "col"), P("row", "col", None), P("row"), P("row"), P("row"))
    groups = mesh.shape["row"]
    if groups == 4 and mesh.shape["col"] == 8:
        body = functools.partial(on_line, groups)
    else:
        body = on_device
    return jax.shard_map(
        body, mesh=mesh, in_specs=placed, out_specs=P("row", None, "col"), check_vma=False
    )
```

profile of v0, /device:TPU:0, one launch (start us, length us, event | category | flops | bytes accessed | tf_op | source)
XLA Modules:
  0.0 121.4 jit_solution(3596605832790711143)
XLA Ops:
  0.0 0.0 copy-start
  0.0 1.6 %copy-done = bf16[8,128,1024]{2,1,0:T(8,128)(2,1)S(1)} copy-done((bf16[8,128,1024]{2,1,0:T(8,128)(2,1)S(1)}, bf16[8,128,1024]{2,1,0:T(8,128)(2,1)}, u32[]{:S(2)}) %copy-start) | copy-done | bytes 2097176
  1.6 0.0 copy-start.1
  1.6 1.4 %copy-done.1 = bf16[2,1024,384]{2,1,0:T(8,128)(2,1)S(1)} copy-done((bf16[2,1024,384]{2,1,0:T(8,128)(2,1)S(1)}, bf16[2,1024,384]{2,1,0:T(8,128)(2,1)}, u32[]{:S(2)}) %copy-start.1) | copy-done | bytes 1572888
  3.0 0.0 copy-start.2
  3.0 0.7 copy-done.2
  3.7 0.0 copy-start.3
  3.7 0.7 copy-done.3
  4.3 0.0 copy-start.4
  4.3 0.7 copy-done.4
  5.0 112.6 %shard_map.55 = f32[2,1024,384]{2,1,0:T(8,128)} custom-call(s32[8]{0:T(128)S(1)} %copy-done.2, s32[8]{0:T(128)S(1)} %copy-done.3, s32[8]{0:T(128)S(1)} %copy-done.4, bf16[2,1024,384]{2,1,0:T(8,128)(2,1)S(1)} %copy-done.1, bf16[8,128,1024]{2,1,0:T(8,128)(2,1)S(1)} %copy-done), custom_call_target="tpu_custom_call" | custom-call | flops 6442450944 | bytes 16777216 | tf_op jit(solution)/shard_map/pallas_call | solution.py:205
  117.6 3.8 %copy.7 = f32[2,1024,384]{2,1,0:T(8,128)} copy(f32[2,1024,384]{2,1,0:T(8,128)} %shard_map.55) | data formatting | bytes 6291456
Async XLA Ops:
  0.0 1.6 %copy-start = (bf16[8,128,1024]{2,1,0:T(8,128)(2,1)S(1)}, bf16[8,128,1024]{2,1,0:T(8,128)(2,1)}, u32[]{:S(2)}) copy-start(bf16[8,128,1024]{2,1,0:T(8,128)(2,1)} %integ.1) | copy-start | bytes 6291460
  1.6 1.4 %copy-start.1 = (bf16[2,1024,384]{2,1,0:T(8,128)(2,1)S(1)}, bf16[2,1024,384]{2,1,0:T(8,128)(2,1)}, u32[]{:S(2)}) copy-start(bf16[2,1024,384]{2,1,0:T(8,128)(2,1)} %amp.1) | copy-start | bytes 4718596
  3.0 0.7 copy-start.2
  3.7 0.7 copy-start.3
  4.3 0.7 copy-start.4
where the time goes:
time: 122 us; the launch traced here: 121 us
  Pallas kernels  113 us (93%)
  local copies, waits for them, and re-layouts  8.72 us (7%)
    pallas_call x1, Pallas kernels, on_line(): pl.pallas_call(functools.partial(line_kernel, groups), out_shape=jax.Shap...  113 us
    unnamed x11, local copies, waits for them, and re-layouts  8.72 us

commit v1 on v0

--- a/solution.py
+++ b/solution.py
@@ -12,7 +12,8 @@
 ROW_TILE = 256
 
 
-def line_kernel(groups, source, target, mask, amp, integ, out, table, own, u1, u2, u3, d1, d2, d3,
+def line_kernel(groups, source_hbm, target_hbm, mask_hbm, amp, integ, out, source, target, mask, table, own,
+                u1, u2, d1, d2, far_head, far_tail, part, scalar_sem,
                 local_sem, isend, irecv, usend, urecv, dsend, drecv):
     z = lax.axis_index("row")
     col = lax.axis_index("col")
@@ -43,17 +44,26 @@
     own_rows = table.at[:, pl.ds(col * rows, rows), :]
     fetch_i = pltpu.make_async_copy(integ, own_rows, local_sem.at[0])
     fetch_a = pltpu.make_async_copy(amp, own, local_sem.at[1])
+    scalars = [
+        pltpu.make_async_copy(src, dst, scalar_sem.at[i])
+        for i, (src, dst) in enumerate(((source_hbm, source), (target_hbm, target), (mask_hbm, mask)))
+    ]
     fetch_i.start()
     fetch_a.start()
+    for scalar in scalars:
+        scalar.start()
     pl.semaphore_wait(barrier, 3 + jnp.where(low, 1, 0) + jnp.where(high, 1, 0))
 
-    per_tile = CHUNKS // pairs
-    chunk_rows = depth // per_tile
+    chunk_rows = depth // CHUNKS
 
     def piece(ref, q):
-        return ref.at[q // per_tile, pl.ds((q % per_tile) * chunk_rows, chunk_rows), :]
-
-    ups, downs = (own, u1, u2, u3), (own, d1, d2, d3)
+        if ref is None:
+            if q == CHUNKS - 1:
+                return far_tail
+            ref = far_head
+        return ref.at[:, pl.ds(q * chunk_rows, chunk_rows), :]
+
+    ups, downs = (own, u1, u2, None), (own, d1, d2, None)
 
     def up(d, q):
         src = amp if d == 1 else ups[d - 1]
@@ -149,17 +159,24 @@
     for i in (0, 7, 8, 9, 10, 11, 12):
         moves[i].wait_recv()
 
-    def contract(tiles, group):
+    for scalar in scalars:
+        scalar.wait()
+
+    def slots_of(group):
         first = jnp.int32(slots)
         last = jnp.int32(-1)
         for k in range(slots):
             match = source[k] // pairs == group
             first = jnp.where(match, jnp.minimum(first, k), first)
             last = jnp.where(match, jnp.maximum(last, k), last)
+        found = []
         for k in (first, last):
             k = jnp.clip(k, 0, slots - 1)
-            tile = source[k] % pairs
-            goal = jnp.where(mask[k] > 0, target[k], -1)
+            found.append((k, source[k] % pairs, jnp.where(mask[k] > 0, target[k], -1)))
+        return found
+
+    def contract(tiles, group):
+        for k, tile, goal in slots_of(group):
 
             @pl.loop(0, depth // ROW_TILE)
             def _(r):
@@ -170,11 +187,7 @@
                     out[p, span, :] += jnp.where(goal == p, product, 0.0)
 
     contract(own, z)
-    for d in range(1, groups):
-        if d == groups - 1:
-            for q in range(CHUNKS):
-                pass_on(d, q)
-
+    for d in range(1, groups - 1):
         @pl.when(z >= d)
         def _():
             contract(ups[d], z - d)
@@ -182,6 +195,37 @@
         @pl.when(z + d < groups)
         def _():
             contract(downs[d], z + d)
+
+    last_hop = groups - 1
+    for q in range(CHUNKS - 1):
+        pass_on(last_hop, q)
+    head = depth - chunk_rows
+    outer = (z == 0) | (z == groups - 1)
+
+    @pl.when(outer)
+    def _():
+        for n, (k, tile, _) in enumerate(slots_of(groups - 1 - z)):
+            @pl.loop(0, depth // ROW_TILE)
+            def _(r):
+                span = pl.ds(pl.multiple_of(r * ROW_TILE, ROW_TILE), ROW_TILE)
+                part[n, span, :] = jnp.dot(
+                    table[k, span, :head], far_head[tile], preferred_element_type=jnp.float32)
+
+    pass_on(last_hop, CHUNKS - 1)
+
+    @pl.when(outer)
+    def _():
+        found = slots_of(groups - 1 - z)
+        for r in range(depth // ROW_TILE):
+            span = slice(r * ROW_TILE, (r + 1) * ROW_TILE)
+            totals = [out[p, span, :] for p in range(pairs)]
+            for n, (k, tile, goal) in enumerate(found):
+                product = part[n, span, :] + jnp.dot(
+                    table[k, span, head:], far_tail[tile], preferred_element_type=jnp.float32)
+                product = product.astype(jnp.bfloat16).astype(jnp.float32)
+                totals = [total + jnp.where(goal == p, product, 0.0) for p, total in enumerate(totals)]
+            for p in range(pairs):
+                out[p, span, :] = totals[p]
 
     for move in moves:
         move.wait_send()
@@ -204,12 +248,19 @@
     hops = (groups - 1) * CHUNKS
     return pl.pallas_call(
         functools.partial(line_kernel, groups),
-        out_shape=jax.ShapeDtypeStruct((pairs, depth, width), jnp.float32),
-        in_specs=[pl.BlockSpec(memory_space=pltpu.SMEM)] * 3 + [pl.BlockSpec(memory_space=pl.ANY)] * 2,
+        out_shape=pltpu.VMEM((pairs, depth, width), jnp.float32),
+        in_specs=[pl.BlockSpec(memory_space=pltpu.HBM)] * 5,
         out_specs=pl.BlockSpec(memory_space=pltpu.VMEM),
         scratch_shapes=[
+            pltpu.SMEM((slots,), jnp.int32),
+            pltpu.SMEM((slots,), jnp.int32),
+            pltpu.SMEM((slots,), jnp.int32),
             pltpu.VMEM((slots, rows * across, inner), integrals.dtype),
-            shard, shard, shard, shard, shard, shard, shard,
+            shard, shard, shard, shard, shard,
+            pltpu.VMEM((pairs, depth - depth // CHUNKS, width), amplitudes.dtype),
+            pltpu.VMEM((pairs, depth // CHUNKS, width), amplitudes.dtype),
+            pltpu.VMEM((2, depth, width), jnp.float32),
+            pltpu.SemaphoreType.DMA((3,)),
             pltpu.SemaphoreType.DMA((2,)),
             pltpu.SemaphoreType.DMA((13,)),
             pltpu.SemaphoreType.DMA((13,)),
@@ -219,7 +270,7 @@
             pltpu.SemaphoreType.DMA((hops,)),
         ],
         compiler_params=pltpu.CompilerParams(
-            collective_id=0, has_side_effects=True, vmem_limit_bytes=48 * 1024 * 1024
+            collective_id=0, has_side_effects=True, vmem_limit_bytes=60 * 1024 * 1024
         ),
         cost_estimate=pl.CostEstimate(
             flops=2 * slots * depth * inner * width, bytes_accessed=16 * 1024 * 1024, transcendentals=0

time: 122 us -> 110 us (0.902)
  local copies, waits for them, and re-layouts: 8.72 us -> 1.67 us
  Pallas kernels: 113 us -> 108 us
    unnamed x11 -> x1, local copies, waits for them, and re-layouts: 8.72 us -> 1.67 us
    pallas_call x1, Pallas kernels: 113 us -> 108 us  [on_line(): pl.pallas_call(functools.partial(line_kernel, groups), out_shape=pltpu.VM...]
where the time goes in v1:
time: 110 us
  Pallas kernels  108 us (98%)
  local copies, waits for them, and re-layouts  1.67 us (2%)
    pallas_call x1, Pallas kernels, on_line(): pl.pallas_call(functools.partial(line_kernel, groups), out_shape=pltpu.VM...  108 us

profile of v1, /device:TPU:0, one launch (start us, length us, event | category | flops | bytes accessed | tf_op | source)
XLA Modules:
  0.0 109.7 jit_solution(12326144564496624087)
XLA Ops:
  0.0 108.0 %shard_map.55 = f32[2,1024,384]{2,1,0:T(8,128)S(1)} custom-call(s32[8]{0:T(128)} %source_hbm.1, s32[8]{0:T(128)} %target_hbm.1, s32[8]{0:T(128)} %mask_hbm.1, bf16[2,1024,384]{2,1,0:T(8,128)(2,1)} %amp.1, bf16[8,128,1024]{2,1,0:T(8,128)(2,1)} %integ.1), custom_call_target="tpu_custom_call" | custom-call | flops 6442450944 | bytes 16777216 | tf_op jit(solution)/shard_map/pallas_call | solution.py:249
  108.0 1.7 %copy.7 = f32[2,1024,384]{2,1,0:T(8,128)} copy(f32[2,1024,384]{2,1,0:T(8,128)S(1)} %shard_map.55) | data formatting | bytes 6291456

commit v2 on v1

--- a/solution.py
+++ b/solution.py
@@ -9,6 +9,7 @@
 
 MESH = pl.DeviceIdType.MESH
 CHUNKS = 4
+IN_FLIGHT = 2
 ROW_TILE = 256
 
 
@@ -120,6 +121,8 @@
             if d < groups - 1:
                 @pl.when(high)
                 def _():
+                    if d + 1 == groups - 1 and q >= IN_FLIGHT:
+                        up(d + 1, q - IN_FLIGHT).wait_send()
                     up(d + 1, q).start()
 
         @pl.when(z + d < groups)
@@ -128,6 +131,8 @@
             if d < groups - 1:
                 @pl.when(low)
                 def _():
+                    if d + 1 == groups - 1 and q >= IN_FLIGHT:
+                        down(d + 1, q - IN_FLIGHT).wait_send()
                     down(d + 1, q).start()
 
     out[...] = jnp.zeros_like(out)
@@ -152,8 +157,6 @@
     moves[11].start()
     moves[6].wait_recv()
     moves[12].start()
-    for q in range(mid, CHUNKS):
-        pass_on(2, q)
     fetch_i.wait()
     fetch_a.wait()
     for i in (0, 7, 8, 9, 10, 11, 12):
@@ -187,7 +190,12 @@
                     out[p, span, :] += jnp.where(goal == p, product, 0.0)
 
     contract(own, z)
+    pass_on(2, mid)
     for d in range(1, groups - 1):
+        if d == 2:
+            for q in range(mid + 1, CHUNKS):
+                pass_on(2, q)
+
         @pl.when(z >= d)
         def _():
             contract(ups[d], z - d)
@@ -230,7 +238,7 @@
     for move in moves:
         move.wait_send()
     for d in range(1, groups):
-        for q in range(CHUNKS):
+        for q in range(CHUNKS - IN_FLIGHT if d == last_hop else 0, CHUNKS):
             @pl.when(high & (z >= d - 1))
             def _():
                 up(d, q).wait_send()

time: 110 us -> 110 us (level)
  no operation moved by 1% of the time
where the time goes in v2:
time: 110 us
  Pallas kernels  108 us (98%)
  local copies, waits for them, and re-layouts  1.67 us (2%)
    pallas_call x1, Pallas kernels, on_line(): pl.pallas_call(functools.partial(line_kernel, groups), out_shape=pltpu.VM...  108 us

profile of v2, /device:TPU:0, one launch (start us, length us, event | category | flops | bytes accessed | tf_op | source)
XLA Modules:
  0.0 109.7 jit_solution(9543460482924381663)
XLA Ops:
  0.0 108.0 %shard_map.55 = f32[2,1024,384]{2,1,0:T(8,128)S(1)} custom-call(s32[8]{0:T(128)} %source_hbm.1, s32[8]{0:T(128)} %target_hbm.1, s32[8]{0:T(128)} %mask_hbm.1, bf16[2,1024,384]{2,1,0:T(8,128)(2,1)} %amp.1, bf16[8,128,1024]{2,1,0:T(8,128)(2,1)} %integ.1), custom_call_target="tpu_custom_call" | custom-call | flops 6442450944 | bytes 16777216 | tf_op jit(solution)/shard_map/pallas_call | solution.py:257
  108.0 1.7 %copy.7 = f32[2,1024,384]{2,1,0:T(8,128)} copy(f32[2,1024,384]{2,1,0:T(8,128)S(1)} %shard_map.55) | data formatting | bytes 6291456

commit v3 on v1

--- a/solution.py
+++ b/solution.py
@@ -9,11 +9,12 @@
 
 MESH = pl.DeviceIdType.MESH
 CHUNKS = 4
+TAIL_SHARE = 8
 ROW_TILE = 256
 
 
 def line_kernel(groups, source_hbm, target_hbm, mask_hbm, amp, integ, out, source, target, mask, table, own,
-                u1, u2, d1, d2, far_head, far_tail, part, scalar_sem,
+                u1, u2, d1, d2, far_head, far_tail, picked, scalar_sem,
                 local_sem, isend, irecv, usend, urecv, dsend, drecv):
     z = lax.axis_index("row")
     col = lax.axis_index("col")
@@ -54,14 +55,17 @@
         scalar.start()
     pl.semaphore_wait(barrier, 3 + jnp.where(low, 1, 0) + jnp.where(high, 1, 0))
 
-    chunk_rows = depth // CHUNKS
+    tail = depth // TAIL_SHARE
+    head = depth - tail
+    chunk_rows = depth * 5 // 16
+    starts = [chunk_rows * q for q in range(CHUNKS - 1)] + [head, depth]
 
     def piece(ref, q):
         if ref is None:
             if q == CHUNKS - 1:
                 return far_tail
             ref = far_head
-        return ref.at[:, pl.ds(q * chunk_rows, chunk_rows), :]
+        return ref.at[:, pl.ds(starts[q], starts[q + 1] - starts[q]), :]
 
     ups, downs = (own, u1, u2, None), (own, d1, d2, None)
 
@@ -199,33 +203,30 @@
     last_hop = groups - 1
     for q in range(CHUNKS - 1):
         pass_on(last_hop, q)
-    head = depth - chunk_rows
     outer = (z == 0) | (z == groups - 1)
 
     @pl.when(outer)
     def _():
-        for n, (k, tile, _) in enumerate(slots_of(groups - 1 - z)):
+        for n, (k, tile, goal) in enumerate(slots_of(groups - 1 - z)):
             @pl.loop(0, depth // ROW_TILE)
             def _(r):
                 span = pl.ds(pl.multiple_of(r * ROW_TILE, ROW_TILE), ROW_TILE)
-                part[n, span, :] = jnp.dot(
-                    table[k, span, :head], far_head[tile], preferred_element_type=jnp.float32)
+                product = jnp.dot(table[k, span, :head], far_head[tile], preferred_element_type=jnp.float32)
+                rest = table[k, span, head:]
+                for p in range(pairs):
+                    out[p, span, :] += jnp.where(goal == p, product, 0.0)
+                    picked[p, span, n * tail:(n + 1) * tail] = jnp.where(goal == p, rest, jnp.zeros_like(rest))
 
     pass_on(last_hop, CHUNKS - 1)
 
     @pl.when(outer)
     def _():
-        found = slots_of(groups - 1 - z)
-        for r in range(depth // ROW_TILE):
-            span = slice(r * ROW_TILE, (r + 1) * ROW_TILE)
-            totals = [out[p, span, :] for p in range(pairs)]
-            for n, (k, tile, goal) in enumerate(found):
-                product = part[n, span, :] + jnp.dot(
-                    table[k, span, head:], far_tail[tile], preferred_element_type=jnp.float32)
-                product = product.astype(jnp.bfloat16).astype(jnp.float32)
-                totals = [total + jnp.where(goal == p, product, 0.0) for p, total in enumerate(totals)]
-            for p in range(pairs):
-                out[p, span, :] = totals[p]
+        last_tiles = [far_tail[tile] for _, tile, _ in slots_of(groups - 1 - z)]
+        rest = jnp.concatenate(last_tiles, axis=0)
+        for p in range(pairs):
+            for r in range(depth // ROW_TILE):
+                span = slice(r * ROW_TILE, (r + 1) * ROW_TILE)
+                out[p, span, :] += jnp.dot(picked[p, span, :], rest, preferred_element_type=jnp.float32)
 
     for move in moves:
         move.wait_send()
@@ -257,9 +258,9 @@
             pltpu.SMEM((slots,), jnp.int32),
             pltpu.VMEM((slots, rows * across, inner), integrals.dtype),
             shard, shard, shard, shard, shard,
-            pltpu.VMEM((pairs, depth - depth // CHUNKS, width), amplitudes.dtype),
-            pltpu.VMEM((pairs, depth // CHUNKS, width), amplitudes.dtype),
-            pltpu.VMEM((2, depth, width), jnp.float32),
+            pltpu.VMEM((pairs, depth - depth // TAIL_SHARE, width), amplitudes.dtype),
+            pltpu.VMEM((pairs, depth // TAIL_SHARE, width), amplitudes.dtype),
+            pltpu.VMEM((pairs, depth, 2 * (depth // TAIL_SHARE)), integrals.dtype),
             pltpu.SemaphoreType.DMA((3,)),
             pltpu.SemaphoreType.DMA((2,)),
             pltpu.SemaphoreType.DMA((13,)),

time: 110 us -> 110 us (level)
  no operation moved by 1% of the time
where the time goes in v3:
time: 110 us
  Pallas kernels  108 us (98%)
  local copies, waits for them, and re-layouts  1.67 us (2%)
    pallas_call x1, Pallas kernels, on_line(): pl.pallas_call(functools.partial(line_kernel, groups), out_shape=pltpu.VM...  108 us

profile of v3, /device:TPU:0, one launch (start us, length us, event | category | flops | bytes accessed | tf_op | source)
XLA Modules:
  0.0 109.9 jit_solution(13515667773469800779)
XLA Ops:
  0.0 108.2 %shard_map.55 = f32[2,1024,384]{2,1,0:T(8,128)S(1)} custom-call(s32[8]{0:T(128)} %source_hbm.1, s32[8]{0:T(128)} %target_hbm.1, s32[8]{0:T(128)} %mask_hbm.1, bf16[2,1024,384]{2,1,0:T(8,128)(2,1)} %amp.1, bf16[8,128,1024]{2,1,0:T(8,128)(2,1)} %integ.1), custom_call_target="tpu_custom_call" | custom-call | flops 6442450944 | bytes 16777216 | tf_op jit(solution)/shard_map/pallas_call | solution.py:250
  108.2 1.7 %copy.7 = f32[2,1024,384]{2,1,0:T(8,128)} copy(f32[2,1024,384]{2,1,0:T(8,128)S(1)} %shard_map.55) | data formatting | bytes 6291456

commit v4 on v1

--- a/solution.py
+++ b/solution.py
@@ -9,7 +9,7 @@
 
 MESH = pl.DeviceIdType.MESH
 CHUNKS = 4
-ROW_TILE = 256
+ROW_TILE = 512
 
 
 def line_kernel(groups, source_hbm, target_hbm, mask_hbm, amp, integ, out, source, target, mask, table, own,

time: 110 us -> 110 us (level)
  no operation moved by 1% of the time
where the time goes in v4:
time: 110 us
  Pallas kernels  108 us (98%)
  local copies, waits for them, and re-layouts  1.67 us (2%)
    pallas_call x1, Pallas kernels, on_line(): pl.pallas_call(functools.partial(line_kernel, groups), out_shape=pltpu.VM...  108 us

profile of v4, /device:TPU:0, one launch (start us, length us, event | category | flops | bytes accessed | tf_op | source)
XLA Modules:
  0.0 109.7 jit_solution(14774795308801342222)
XLA Ops:
  0.0 108.0 %shard_map.55 = f32[2,1024,384]{2,1,0:T(8,128)S(1)} custom-call(s32[8]{0:T(128)} %source_hbm.1, s32[8]{0:T(128)} %target_hbm.1, s32[8]{0:T(128)} %mask_hbm.1, bf16[2,1024,384]{2,1,0:T(8,128)(2,1)} %amp.1, bf16[8,128,1024]{2,1,0:T(8,128)(2,1)} %integ.1), custom_call_target="tpu_custom_call" | custom-call | flops 6442450944 | bytes 16777216 | tf_op jit(solution)/shard_map/pallas_call | solution.py:249
  108.0 1.7 %copy.7 = f32[2,1024,384]{2,1,0:T(8,128)} copy(f32[2,1024,384]{2,1,0:T(8,128)S(1)} %shard_map.55) | data formatting | bytes 6291456
